TPU v7x, 32 devices: a whole 2x2x4 slice. The times are simulated.
32 devices in a mesh: groups: 2 (over x), dp: 16 (over z, y, core).
Axes of the slice: x: 2, y: 2, z: 4, core: 2. Of those that a mesh axis runs over, the one named last changes fastest.
Arguments:
- points: float32 [32, 32768], P(None, ('groups', 'dp')), parts along dimension 1, may hold values from -6 to 6
- centres: float32 [32, 8192], P(None, ('groups', 'dp')), parts along dimension 1, may hold values from -6 to 6
- direction: float32 [8192], P(('groups', 'dp')), parts along dimension 0, may hold values from -6 to 6
- counts: int32 [32], P(('groups', 'dp')), parts along dimension 0, may hold values from 256 to 1024, as said below
Outputs:
- product: float32 [8192], P(('groups', 'dp')), parts along dimension 0
There are 2 independent parts, one for each index of `groups`. A program takes and returns all parts, laid end to end along the dimension named above; each array names one. Nothing has to cross between parts.
Inputs may be any that keep to these rules, and one draw needn't show every extreme that they name: `counts`: some index holds exactly 1024 live slots and some other exactly 256.
All inputs are finite; a program needn't handle non-finite values.
Results may differ from a plain program's by a relative error of at most 0.0003.
Values sent between devices are 32-bit elements; how exact they have to be, the bound alone decides.
A program may use at most 64 MiB of HBM per device.

v0:
```python
import jax
import jax.numpy as jnp
from jax import lax
from jax.sharding import PartitionSpec as P


def kernel_rows(pts, cen, cen_norm):
    cross = lax.dot_general(
        pts,
        cen,
        (((0,), (0,)), ((), ())),
        precision=lax.Precision.HIGHEST,
        preferred_element_type=jnp.float32,
    )
    pts_norm = jnp.sum(pts * pts, axis=0)
    dist = pts_norm[:, None] + cen_norm[None, :] - 2.0 * cross
    return jnp.exp(-dist / pts.shape[0]).astype(jnp.bfloat16)


def kern_times(kern, vdir):
    return jnp.dot(
        kern.astype(jnp.float32),
        vdir,
        precision=lax.Precision.HIGHEST,
        preferred_element_type=jnp.float32,
    )


def body(points, centres, direction, counts):
    width, slots_dev = points.shape
    cen_dev = centres.shape[1]
    ndev = lax.axis_size("dp")
    count_m = cen_dev * ndev
    blk = min(128, slots_dev)
    scale_m = 1.0 / jnp.sqrt(jnp.float32(count_m))
    live_count = counts[0]
    dir_row = direction.reshape(1, cen_dev)
    all_cen, all_dir = (
        lax.all_gather(centres, "dp", axis=1, tiled=True),
        lax.all_gather(dir_row, "dp", axis=1, tiled=True),
    )
    cen_norm = jnp.sum(all_cen * all_cen, axis=0)
    vdir = all_dir[0]

    def one_block(index, acc):
        pts = lax.dynamic_slice_in_dim(points, index * blk, blk, 1)
        kern = kernel_rows(pts, all_cen, cen_norm)
        rows = index * blk + jnp.arange(blk, dtype=jnp.int32)
        inner = kern_times(kern, vdir) * scale_m
        inner = jnp.where(rows < live_count, inner, jnp.float32(0.0)).astype(jnp.bfloat16)
        return acc + jnp.dot(inner, kern, preferred_element_type=jnp.float32)

    start_acc = jnp.zeros((count_m,), jnp.float32)
    terms = lax.fori_loop(0, slots_dev // blk, one_block, start_acc)
    summed = lax.psum_scatter(terms, "dp", scatter_dimension=0, tiled=True)
    return summed / jnp.sqrt(jnp.float32(slots_dev * ndev))


def solution(mesh):
    placed = (
        P(None, ("groups", "dp")),
        P(None, ("groups", "dp")),
        P(("groups", "dp")),
        P(("groups", "dp")),
    )
    return jax.shard_map(
        body, mesh=mesh, in_specs=placed, out_specs=P(("groups", "dp")), check_vma=False
    )
```

profile of v0, /device:TPU:0, one launch (start us, length us, event | category | flops | bytes accessed | tf_op | source)
XLA Modules:
  0.0 147.5 jit_solution(12265100108171049449)
XLA Ops:
  0.0 24.9 %all_gather.6 = f32[32,4096]{1,0:T(8,128)S(1)} all-gather(f32[32,256]{1,0:T(8,128)} %param.7), channel_id=1, replica_groups=mesh['groups'=2,'dp'=16] {'dp'}, dimensions={1}, use_global_device_ids=true | all-gather | bytes 557056 | tf_op jit(solution)/shard_map/all_gather | solution.py:39
  25.0 17.5 %all-gather.1 = f32[16,1,256]{2,1,0:T(1,128)S(1)} all-gather(f32[1,1,256]{2,1,0:T(1,128)S(1)} %bitcast.44), channel_id=2, replica_groups=mesh['groups'=2,'dp'=16] {'dp'}, dimensions={0}, use_global_device_ids=true | all-gather | bytes 17408 | tf_op jit(solution)/shard_map/all_gather | solution.py:40
  42.4 44.1 %while.14 = (s32[]{:T(128)}, f32[4096]{0:T(1024)S(1)}, s32[]{:T(128)}, f32[32,1024]{1,0:T(8,128)}, f32[4096]{0:T(1024)S(1)}, /*index=5*/f32[32,4096]{1,0:T(8,128...) while((s32[]{:T(128)}, f32[4096]{0:T(1024)S(1)}, s32[]{:T(128)}, ...), condition=%wide.region_3.4_spmd.clone, body=%wide.region_1.3_spmd.clone.sunk | while | flops 211829248 | bytes 3802805 | solution.py:54
  42.4 0.7 multiply_reduce_fusion.3
  43.2 2.9 %fusion.32 = bf16[128,4096]{1,0:T(8,128)(2,1)S(1)} fusion(f32[32,4096]{1,0:T(8,128)S(1)} %get-tuple-element.238, f32[4096]{0:T(1024)S(1)} %get-tuple-element.237, f32[128]{0:T(128)S(1)} %multiply_reduce_fusion.3, f32[32,1024]{1,0:T(8,128)} %get-tuple-element.236, s32[]{:T(128)S(6)} %select_n.25), kind=kOutput, calls=%fused_computation.5.clone.1 | convolution fusion | flops 204472320 | bytes 1606148 | tf_op jit(solution)/shard_map/while/body/eval_jaxpr/dot_general | solution.py:8
  46.1 1.6 %fusion.33 = bf16[128,1]{0,1:T(2,128)(2,1)S(1)} fusion(bf16[128,4096]{1,0:T(8,128)(2,1)S(1)} %fusion.32, f32[4096,1]{0,1:T(1,128)S(1)} %bitcast.43, s32[]{:T(128)} %get-tuple-element.235, s32[]{:T(128)S(6)} %mul.64), kind=kOutput, calls=%fused_computation.10.clone.1 | convolution fusion | flops 6292096 | bytes 1065224 | tf_op jit(solution)/shard_map/while/body/eval_jaxpr/dot_general | solution.py:21
  47.7 0.3 fusion.34
  48.0 0.7 multiply_reduce_fusion.3
  48.7 2.9 %fusion.32 = bf16[128,4096]{1,0:T(8,128)(2,1)S(1)} fusion(f32[32,4096]{1,0:T(8,128)S(1)} %get-tuple-element.238, f32[4096]{0:T(1024)S(1)} %get-tuple-element.237, f32[128]{0:T(128)S(1)} %multiply_reduce_fusion.3, f32[32,1024]{1,0:T(8,128)} %get-tuple-element.236, s32[]{:T(128)S(6)} %select_n.25), kind=kOutput, calls=%fused_computation.5.clone.1 | convolution fusion | flops 204472320 | bytes 1606148 | tf_op jit(solution)/shard_map/while/body/eval_jaxpr/dot_general | solution.py:8
  51.6 1.6 %fusion.33 = bf16[128,1]{0,1:T(2,128)(2,1)S(1)} fusion(bf16[128,4096]{1,0:T(8,128)(2,1)S(1)} %fusion.32, f32[4096,1]{0,1:T(1,128)S(1)} %bitcast.43, s32[]{:T(128)} %get-tuple-element.235, s32[]{:T(128)S(6)} %mul.64), kind=kOutput, calls=%fused_computation.10.clone.1 | convolution fusion | flops 6292096 | bytes 1065224 | tf_op jit(solution)/shard_map/while/body/eval_jaxpr/dot_general | solution.py:21
  53.2 0.3 fusion.34
  53.5 0.7 multiply_reduce_fusion.3
  54.2 2.9 %fusion.32 = bf16[128,4096]{1,0:T(8,128)(2,1)S(1)} fusion(f32[32,4096]{1,0:T(8,128)S(1)} %get-tuple-element.238, f32[4096]{0:T(1024)S(1)} %get-tuple-element.237, f32[128]{0:T(128)S(1)} %multiply_reduce_fusion.3, f32[32,1024]{1,0:T(8,128)} %get-tuple-element.236, s32[]{:T(128)S(6)} %select_n.25), kind=kOutput, calls=%fused_computation.5.clone.1 | convolution fusion | flops 204472320 | bytes 1606148 | tf_op jit(solution)/shard_map/while/body/eval_jaxpr/dot_general | solution.py:8
  57.1 1.6 %fusion.33 = bf16[128,1]{0,1:T(2,128)(2,1)S(1)} fusion(bf16[128,4096]{1,0:T(8,128)(2,1)S(1)} %fusion.32, f32[4096,1]{0,1:T(1,128)S(1)} %bitcast.43, s32[]{:T(128)} %get-tuple-element.235, s32[]{:T(128)S(6)} %mul.64), kind=kOutput, calls=%fused_computation.10.clone.1 | convolution fusion | flops 6292096 | bytes 1065224 | tf_op jit(solution)/shard_map/while/body/eval_jaxpr/dot_general | solution.py:21
  59.0 0.7 multiply_reduce_fusion.3
  59.7 2.9 %fusion.32 = bf16[128,4096]{1,0:T(8,128)(2,1)S(1)} fusion(f32[32,4096]{1,0:T(8,128)S(1)} %get-tuple-element.238, f32[4096]{0:T(1024)S(1)} %get-tuple-element.237, f32[128]{0:T(128)S(1)} %multiply_reduce_fusion.3, f32[32,1024]{1,0:T(8,128)} %get-tuple-element.236, s32[]{:T(128)S(6)} %select_n.25), kind=kOutput, calls=%fused_computation.5.clone.1 | convolution fusion | flops 204472320 | bytes 1606148 | tf_op jit(solution)/shard_map/while/body/eval_jaxpr/dot_general | solution.py:8
  62.6 1.6 %fusion.33 = bf16[128,1]{0,1:T(2,128)(2,1)S(1)} fusion(bf16[128,4096]{1,0:T(8,128)(2,1)S(1)} %fusion.32, f32[4096,1]{0,1:T(1,128)S(1)} %bitcast.43, s32[]{:T(128)} %get-tuple-element.235, s32[]{:T(128)S(6)} %mul.64), kind=kOutput, calls=%fused_computation.10.clone.1 | convolution fusion | flops 6292096 | bytes 1065224 | tf_op jit(solution)/shard_map/while/body/eval_jaxpr/dot_general | solution.py:21
  64.5 0.7 multiply_reduce_fusion.3
  65.2 2.9 %fusion.32 = bf16[128,4096]{1,0:T(8,128)(2,1)S(1)} fusion(f32[32,4096]{1,0:T(8,128)S(1)} %get-tuple-element.238, f32[4096]{0:T(1024)S(1)} %get-tuple-element.237, f32[128]{0:T(128)S(1)} %multiply_reduce_fusion.3, f32[32,1024]{1,0:T(8,128)} %get-tuple-element.236, s32[]{:T(128)S(6)} %select_n.25), kind=kOutput, calls=%fused_computation.5.clone.1 | convolution fusion | flops 204472320 | bytes 1606148 | tf_op jit(solution)/shard_map/while/body/eval_jaxpr/dot_general | solution.py:8
  68.2 1.6 %fusion.33 = bf16[128,1]{0,1:T(2,128)(2,1)S(1)} fusion(bf16[128,4096]{1,0:T(8,128)(2,1)S(1)} %fusion.32, f32[4096,1]{0,1:T(1,128)S(1)} %bitcast.43, s32[]{:T(128)} %get-tuple-element.235, s32[]{:T(128)S(6)} %mul.64), kind=kOutput, calls=%fused_computation.10.clone.1 | convolution fusion | flops 6292096 | bytes 1065224 | tf_op jit(solution)/shard_map/while/body/eval_jaxpr/dot_general | solution.py:21
  70.0 0.7 multiply_reduce_fusion.3
  70.7 2.9 %fusion.32 = bf16[128,4096]{1,0:T(8,128)(2,1)S(1)} fusion(f32[32,4096]{1,0:T(8,128)S(1)} %get-tuple-element.238, f32[4096]{0:T(1024)S(1)} %get-tuple-element.237, f32[128]{0:T(128)S(1)} %multiply_reduce_fusion.3, f32[32,1024]{1,0:T(8,128)} %get-tuple-element.236, s32[]{:T(128)S(6)} %select_n.25), kind=kOutput, calls=%fused_computation.5.clone.1 | convolution fusion | flops 204472320 | bytes 1606148 | tf_op jit(solution)/shard_map/while/body/eval_jaxpr/dot_general | solution.py:8
  73.7 1.6 %fusion.33 = bf16[128,1]{0,1:T(2,128)(2,1)S(1)} fusion(bf16[128,4096]{1,0:T(8,128)(2,1)S(1)} %fusion.32, f32[4096,1]{0,1:T(1,128)S(1)} %bitcast.43, s32[]{:T(128)} %get-tuple-element.235, s32[]{:T(128)S(6)} %mul.64), kind=kOutput, calls=%fused_computation.10.clone.1 | convolution fusion | flops 6292096 | bytes 1065224 | tf_op jit(solution)/shard_map/while/body/eval_jaxpr/dot_general | solution.py:21
  75.5 0.7 multiply_reduce_fusion.3
  76.2 2.9 %fusion.32 = bf16[128,4096]{1,0:T(8,128)(2,1)S(1)} fusion(f32[32,4096]{1,0:T(8,128)S(1)} %get-tuple-element.238, f32[4096]{0:T(1024)S(1)} %get-tuple-element.237, f32[128]{0:T(128)S(1)} %multiply_reduce_fusion.3, f32[32,1024]{1,0:T(8,128)} %get-tuple-element.236, s32[]{:T(128)S(6)} %select_n.25), kind=kOutput, calls=%fused_computation.5.clone.1 | convolution fusion | flops 204472320 | bytes 1606148 | tf_op jit(solution)/shard_map/while/body/eval_jaxpr/dot_general | solution.py:8
  79.2 1.6 %fusion.33 = bf16[128,1]{0,1:T(2,128)(2,1)S(1)} fusion(bf16[128,4096]{1,0:T(8,128)(2,1)S(1)} %fusion.32, f32[4096,1]{0,1:T(1,128)S(1)} %bitcast.43, s32[]{:T(128)} %get-tuple-element.235, s32[]{:T(128)S(6)} %mul.64), kind=kOutput, calls=%fused_computation.10.clone.1 | convolution fusion | flops 6292096 | bytes 1065224 | tf_op jit(solution)/shard_map/while/body/eval_jaxpr/dot_general | solution.py:21
  81.0 0.7 multiply_reduce_fusion.3
  81.7 2.9 %fusion.32 = bf16[128,4096]{1,0:T(8,128)(2,1)S(1)} fusion(f32[32,4096]{1,0:T(8,128)S(1)} %get-tuple-element.238, f32[4096]{0:T(1024)S(1)} %get-tuple-element.237, f32[128]{0:T(128)S(1)} %multiply_reduce_fusion.3, f32[32,1024]{1,0:T(8,128)} %get-tuple-element.236, s32[]{:T(128)S(6)} %select_n.25), kind=kOutput, calls=%fused_computation.5.clone.1 | convolution fusion | flops 204472320 | bytes 1606148 | tf_op jit(solution)/shard_map/while/body/eval_jaxpr/dot_general | solution.py:8
  84.7 1.6 %fusion.33 = bf16[128,1]{0,1:T(2,128)(2,1)S(1)} fusion(bf16[128,4096]{1,0:T(8,128)(2,1)S(1)} %fusion.32, f32[4096,1]{0,1:T(1,128)S(1)} %bitcast.43, s32[]{:T(128)} %get-tuple-element.235, s32[]{:T(128)S(6)} %mul.64), kind=kOutput, calls=%fused_computation.10.clone.1 | convolution fusion | flops 6292096 | bytes 1065224 | tf_op jit(solution)/shard_map/while/body/eval_jaxpr/dot_general | solution.py:21
  86.5 59.1 %all-reduce = f32[4096]{0:T(1024)S(1)} all-reduce(f32[4096]{0:T(1024)S(1)} %get-tuple-element.129), channel_id=3, replica_groups=mesh['groups'=2,'dp'=16] {'dp'}, use_global_device_ids=true, to_apply=%region_4.5.clone | all-reduce | flops 4096 | bytes 32768
  145.6 0.6 dynamic-slice
  146.8 0.6 dynamic-slice_multiply_fusion
  (20 shorter events, 1.7 us)
Async XLA Ops:
  0.0 25.0 %copy-start = (f32[256]{0:T(256)S(1)}, f32[256]{0:T(256)}, u32[]{:S(2)}) copy-start(f32[256]{0:T(256)} %param.8) | copy-start | bytes 3076
  42.4 103.1 %copy-start.1 = (u32[32]{0:T(128)S(1)}, u32[32]{0:T(128)}, u32[]{:S(2)}) copy-start(u32[32]{0:T(128)} %constant.64) | copy-start | bytes 388
where the time goes:
time: 149 us; the launch traced here: 147 us
  blocking collectives  101 us (68%)
  matrix products  37.9 us (25%)
  other arithmetic  6.7 us (4%)
    unnamed x1, blocking collectives  59.1 us
    all_gather x1, blocking collectives, body(): lax.all_gather(centres, 'dp', axis=1, tiled=True)  24.9 us
    dot_general x8, matrix products, kernel_rows(): lax.dot_general(pts, cen, (((0,), (0,)), ((), ())), precision=lax.Precisi...  23.4 us
    all_gather x1, blocking collectives, body(): lax.all_gather(dir_row, 'dp', axis=1, tiled=True)  17.5 us
    dot_general x8, matrix products, kern_times(): jnp.dot(kern.astype(jnp.float32), vdir, precision=lax.Precision.HIGHEST,...  12.5 us
    reduce_sum x8, other arithmetic, kernel_rows(): pts_norm = jnp.sum(pts * pts, axis=0)  5.94 us

commit v1 on v0

v1 whole, which is shorter than its diff:
```python
import functools
import math

import jax
import jax.numpy as jnp
from jax import lax
from jax.experimental import pallas as pl
from jax.experimental.pallas import tpu as pltpu
from jax.sharding import PartitionSpec as P

MESH = pl.DeviceIdType.MESH
KERN_BYTES = 16 << 20
F32, BF16 = jnp.float32, jnp.bfloat16


def split3(x):
    high = x.astype(BF16)
    rest = x - high.astype(F32)
    mid = rest.astype(BF16)
    low = (rest - mid.astype(F32)).astype(BF16)
    return high, mid, low


def rows_of(count, terms):
    columns = terms[0].shape[1]
    at = lax.broadcasted_iota(jnp.int32, (count, columns), 0)
    out = jnp.zeros((count, columns), F32)
    for row, term in enumerate(terms):
        out = jnp.where(at == row, term.astype(F32), out)
    return out.astype(BF16)


def stack_points(pts):
    scale = math.log2(math.e) / pts.shape[0]
    h, m, l = split3(pts)
    norm = jnp.sum(pts * pts, axis=0, keepdims=True) * (-scale)
    one = jnp.ones_like(norm)
    return jnp.concatenate([h, h, m, h, m, l, rows_of(16, [*split3(norm), one, one, one])], axis=0)


def stack_centres(cen):
    scale = math.log2(math.e) / cen.shape[0]
    h, m, l = split3(cen * (2.0 * scale))
    norm = jnp.sum(cen * cen, axis=0, keepdims=True) * (-scale)
    one = jnp.ones_like(norm)
    return jnp.concatenate([h, m, h, l, m, h, rows_of(16, [one, one, one, *split3(norm)])], axis=0)


def kernel(n, nblk, pts, cen, vdir, cnt, out, cbuf, pbuf, kbuf, inn, tbuf, rbuf, gs, gr, fs, ts, tr):
    width, slots = pts.shape
    cen_dev = cen.shape[1]
    blk = slots // nblk
    nch = n // 2
    me = lax.axis_index("dp")
    chip, core = lax.div(me, 2), lax.rem(me, 2)
    sibling = chip * 2 + 1 - core
    paired = nch & (nch - 1) == 0

    def flip(value, s):
        total, bit = 0, 1
        while bit < n:
            a, b = lax.rem(lax.div(value, bit), 2), (s // bit) % 2
            total = total + bit * (a + b - 2 * a * b)
            bit *= 2
        return total

    def chip_to(s):
        return flip(chip, s) if paired else lax.rem(chip + s, nch)

    def chip_from(s):
        return flip(chip, s) if paired else lax.rem(chip + nch - s, nch)

    barrier = pltpu.get_barrier_semaphore()
    for s in range(1, n):
        pl.semaphore_signal(barrier, inc=1, device_id={"dp": lax.rem(me + s, n)}, device_id_type=MESH)

    cbuf[me, :width, :] = cen[...]
    cbuf[me, width:, :] = jnp.concatenate([vdir[...], jnp.zeros((7, cen_dev), F32)], axis=0)
    pbuf[...] = stack_points(pts[...])
    pl.semaphore_wait(barrier, n - 1)

    def send_own(s):
        target = chip_to(s) * 2 + core if not (isinstance(s, int) and s == 0) else sibling
        return pltpu.make_async_remote_copy(
            src_ref=cbuf.at[me], dst_ref=cbuf.at[me], send_sem=gs.at[s], recv_sem=gr.at[me],
            device_id={"dp": target}, device_id_type=MESH)

    def forward(s):
        q = chip_from(s) * 2 + core
        return pltpu.make_async_remote_copy(
            src_ref=cbuf.at[q], dst_ref=cbuf.at[q], send_sem=fs.at[s], recv_sem=gr.at[q],
            device_id={"dp": sibling}, device_id_type=MESH)

    def wait_slot(q):
        pltpu.make_async_remote_copy(
            src_ref=cbuf.at[q], dst_ref=cbuf.at[q], send_sem=gs.at[0], recv_sem=gr.at[q],
            device_id={"dp": sibling}, device_id_type=MESH).wait_recv()

    def loop(start, stop, body):
        if stop - start <= 16:
            for s in range(start, stop):
                body(s)
        else:
            pl.loop(start, stop)(body)

    send_own(0).start()
    loop(1, nch, lambda s: send_own(s).start())

    def one_block(q, columns):
        held = cbuf[q]
        terms = stack_centres(held[:width])
        kern = jnp.exp2(lax.dot_general(
            terms, pbuf[:, columns], (((0,), (0,)), ((), ())), preferred_element_type=F32)).astype(BF16)
        kbuf[q] = kern
        weights = rows_of(16, split3(held[width:width + 1]))
        inn[...] += jnp.dot(weights, kern, preferred_element_type=F32)

    live = cnt[0]
    for part in range(nblk):
        columns = pl.ds(part * blk, blk)
        inn[...] = jnp.zeros_like(inn)
        one_block(me, columns)

        def step(s, part=part, columns=columns):
            near = chip_from(s) * 2 + core
            if part == 0:
                wait_slot(near)
                forward(s).start()
            one_block(near, columns)
            far = chip_from(s - 1) * 2 + 1 - core
            if part == 0:
                wait_slot(far)
            one_block(far, columns)

        loop(1, nch, step)
        last = chip_from(nch - 1) * 2 + 1 - core
        if part == 0:
            wait_slot(last)
        one_block(last, columns)

        sums = jnp.sum(inn[...], axis=0, keepdims=True) * (1.0 / math.sqrt(n * cen_dev))
        at = part * blk + lax.broadcasted_iota(jnp.int32, sums.shape, 1)
        inner = rows_of(16, [jnp.where(at < live, sums, 0.0)])

        def owner(s, part=part, inner=inner):
            q = lax.rem(me + s, n)
            term = lax.dot_general(
                inner, kbuf[q], (((1,), (1,)), ((), ())), preferred_element_type=F32)[:1]
            tbuf[q] = term if part == 0 else tbuf[q] + term
            if part == nblk - 1:
                send_term(s).start()

        def send_term(s):
            q = lax.rem(me + s, n)
            return pltpu.make_async_remote_copy(
                src_ref=tbuf.at[q], dst_ref=rbuf.at[me], send_sem=ts.at[s], recv_sem=tr.at[me],
                device_id={"dp": q}, device_id_type=MESH)

        loop(1, n, owner)
        mine = lax.dot_general(
            inner, kbuf[me], (((1,), (1,)), ((), ())), preferred_element_type=F32)[:1]
        tbuf[me] = mine if part == 0 else tbuf[me] + mine

    loop(0, nch, lambda s: send_own(s).wait_send())
    loop(1, nch, lambda s: forward(s).wait_send())
    out[...] = tbuf[me]

    def gather(s):
        q = lax.rem(me + s, n)
        pltpu.make_async_remote_copy(
            src_ref=tbuf.at[q], dst_ref=rbuf.at[q], send_sem=ts.at[s], recv_sem=tr.at[q],
            device_id={"dp": q}, device_id_type=MESH).wait()
        out[...] += rbuf[q]

    loop(1, n, gather)
    out[...] = out[...] * (1.0 / math.sqrt(slots * n))


def body(n, points, centres, direction, counts):
    width, slots = points.shape
    cen_dev = centres.shape[1]
    nblk = 1
    while n * cen_dev * (slots // nblk) * 2 > KERN_BYTES:
        nblk *= 2
    blk = slots // nblk
    depth = 6 * width + 16
    vmem = pl.BlockSpec(memory_space=pltpu.VMEM)
    got = pl.pallas_call(
        functools.partial(kernel, n, nblk),
        out_shape=jax.ShapeDtypeStruct((1, cen_dev), F32),
        in_specs=[vmem, vmem, vmem, pl.BlockSpec(memory_space=pltpu.SMEM)],
        out_specs=vmem,
        scratch_shapes=[
            pltpu.VMEM((n, width + 8, cen_dev), F32),
            pltpu.VMEM((depth, slots), BF16),
            pltpu.VMEM((n, cen_dev, blk), BF16),
            pltpu.VMEM((16, blk), F32),
            pltpu.VMEM((n, 1, cen_dev), F32),
            pltpu.VMEM((n, 1, cen_dev), F32),
            pltpu.SemaphoreType.DMA((n,)),
            pltpu.SemaphoreType.DMA((n,)),
            pltpu.SemaphoreType.DMA((n,)),
            pltpu.SemaphoreType.DMA((n,)),
            pltpu.SemaphoreType.DMA((n,)),
        ],
        compiler_params=pltpu.CompilerParams(
            collective_id=0, has_side_effects=True, vmem_limit_bytes=48 << 20),
        cost_estimate=pl.CostEstimate(
            flops=2 * slots * n * cen_dev * (depth + 2), bytes_accessed=4 * width * (slots + cen_dev),
            transcendentals=slots * n * cen_dev),
    )(points, centres, direction.reshape(1, cen_dev), counts)
    return got.reshape(cen_dev)


def solution(mesh):
    placed = (
        P(None, ("groups", "dp")),
        P(None, ("groups", "dp")),
        P(("groups", "dp")),
        P(("groups", "dp")),
    )
    return jax.shard_map(
        functools.partial(body, mesh.shape["dp"]), mesh=mesh, in_specs=placed,
        out_specs=P(("groups", "dp")), check_vma=False)
```

time: 149 us -> 29.1 us (0.20)
  blocking collectives: 101 us -> 0 us
  matrix products: 37.9 us -> 0 us
  Pallas kernels: 0 us -> 25.3 us
  other arithmetic: 6.7 us -> 0 us
  local copies, waits for them, and re-layouts: 0.59 us -> 2.9 us
    unnamed x1 -> x0, blocking collectives: 59.1 us -> none
    all_gather x2 -> x0, blocking collectives: 42.4 us -> none  [the longest x1 24.9 us: body(): lax.all_gather(centres, 'dp', axis=1, tiled=True)]
    dot_general x24 -> x0, matrix products: 37.9 us -> none  [the longest x8 23.4 us: kernel_rows(): lax.dot_general(pts, cen, (((0,), (0,)), ((), ())), precision=lax.Precisi...]
    pallas_call x0 -> x1, Pallas kernels: none -> 25.3 us  [body(): pl.pallas_call(functools.partial(kernel, n, nblk), out_shape=jax.ShapeDty...]
    reduce_sum x9 -> x0, other arithmetic: 6 us -> none  [the longest x8 5.94 us: kernel_rows(): pts_norm = jnp.sum(pts * pts, axis=0)]
    unnamed x5 -> x7, local copies, waits for them, and re-layouts: 0.59 us -> 2.9 us
where the time goes in v1:
time: 29.1 us; the launch traced here: 28.9 us
  Pallas kernels  25.3 us (87%)
  local copies, waits for them, and re-layouts  2.9 us (10%)
  between operations  0.67 us (2%)
    pallas_call x1, Pallas kernels, body(): pl.pallas_call(functools.partial(kernel, n, nblk), out_shape=jax.ShapeDty...  25.3 us
    unnamed x7, local copies, waits for them, and re-layouts  2.9 us

profile of v1, /device:TPU:0, one launch (start us, length us, event | category | flops | bytes accessed | tf_op | source)
XLA Modules:
  0.0 28.9 jit_solution(3345362800110281991)
XLA Ops:
  0.7 0.0 copy-start.2
  0.7 0.7 %copy-done.2 = f32[256]{0:T(256)S(1)} copy-done((f32[256]{0:T(256)S(1)}, f32[256]{0:T(256)}, u32[]{:S(2)}) %copy-start.2) | copy-done | bytes 1048
  1.3 0.0 copy-start
  1.3 0.9 %copy-done = f32[32,1024]{1,0:T(8,128)S(1)} copy-done((f32[32,1024]{1,0:T(8,128)S(1)}, f32[32,1024]{1,0:T(8,128)}, u32[]{:S(2)}) %copy-start) | copy-done | bytes 131096
  2.2 0.0 copy-start.1
  2.2 0.8 %copy-done.1 = f32[32,256]{1,0:T(8,128)S(1)} copy-done((f32[32,256]{1,0:T(8,128)S(1)}, f32[32,256]{1,0:T(8,128)}, u32[]{:S(2)}) %copy-start.1) | copy-done | bytes 32792
  3.0 25.3 %shard_map.46 = f32[1,256]{1,0:T(1,128)S(1)} custom-call(f32[32,1024]{1,0:T(8,128)S(1)} %copy-done, f32[32,256]{1,0:T(8,128)S(1)} %copy-done.1, f32[1,256]{1,0:T(1,128)S(1)} %bitcast.3, s32[1]{0:T(128)S(6)} %copy.6.cnt), custom_call_target="tpu_custom_call" | custom-call | flops 1761607680 | bytes 163840 | tf_op jit(solution)/shard_map/pallas_call | solution.py:188
  28.3 0.6 %copy.7 = f32[256]{0:T(256)} copy(f32[256]{0:T(256)S(1)} %bitcast.2) | data formatting | bytes 2048
Async XLA Ops:
  0.7 0.7 %copy-start.2 = (f32[256]{0:T(256)S(1)}, f32[256]{0:T(256)}, u32[]{:S(2)}) copy-start(f32[256]{0:T(256)} %param.6) | copy-start | bytes 3076
  1.3 0.9 %copy-start = (f32[32,1024]{1,0:T(8,128)S(1)}, f32[32,1024]{1,0:T(8,128)}, u32[]{:S(2)}) copy-start(f32[32,1024]{1,0:T(8,128)} %pts.1) | copy-start | bytes 393220
  2.2 0.8 %copy-start.1 = (f32[32,256]{1,0:T(8,128)S(1)}, f32[32,256]{1,0:T(8,128)}, u32[]{:S(2)}) copy-start(f32[32,256]{1,0:T(8,128)} %cen.1) | copy-start | bytes 98308

commit v2 on v1

v2 whole, which is shorter than its diff:
```python
import functools
import math

import jax
import jax.numpy as jnp
from jax import lax
from jax.experimental import pallas as pl
from jax.experimental.pallas import tpu as pltpu
from jax.sharding import PartitionSpec as P

MESH = pl.DeviceIdType.MESH
KERN_BYTES = 16 << 20
F32, BF16 = jnp.float32, jnp.bfloat16


def split3(x):
    high = x.astype(BF16)
    rest = x - high.astype(F32)
    mid = rest.astype(BF16)
    low = (rest - mid.astype(F32)).astype(BF16)
    return high, mid, low


def rows_of(count, terms):
    columns = terms[0].shape[1]
    at = lax.broadcasted_iota(jnp.int32, (count, columns), 0)
    out = jnp.zeros((count, columns), F32)
    for row, term in enumerate(terms):
        out = jnp.where(at == row, term.astype(F32), out)
    return out.astype(BF16)


def stack_points(pts):
    scale = math.log2(math.e) / pts.shape[0]
    h, m, l = split3(pts)
    norm = jnp.sum(pts * pts, axis=0, keepdims=True) * (-scale)
    one = jnp.ones_like(norm)
    return jnp.concatenate([h, h, m, h, m, l, rows_of(16, [*split3(norm), one, one, one])], axis=0)


def stack_centres(cen):
    scale = math.log2(math.e) / cen.shape[0]
    h, m, l = split3(cen * (2.0 * scale))
    norm = jnp.sum(cen * cen, axis=0, keepdims=True) * (-scale)
    one = jnp.ones_like(norm)
    return jnp.concatenate([h, m, h, l, m, h, rows_of(16, [one, one, one, *split3(norm)])], axis=0)


def kernel(nch, nblk, pts, cen, vdir, cnt, out, pshare, cbuf, drow, live, pbuf, kbuf, inn, ibuf, tbuf, rbuf,
           ls, ps, gs, gr, es, er, ts, tr):
    width, slots = pts.shape
    cen_dev = cen.shape[1]
    blk = slots // nblk
    me = lax.axis_index("dp")
    chip, core = lax.div(me, 2), lax.rem(me, 2)
    other = 1 - core
    sibling = {"dp": chip * 2 + other}
    paired = nch & (nch - 1) == 0

    def flip(value, s):
        total, bit = 0, 1
        while bit < nch:
            a, b = lax.rem(lax.div(value, bit), 2), (s // bit) % 2
            total = total + bit * (a + b - 2 * a * b)
            bit *= 2
        return total

    def chip_to(s):
        return flip(chip, s) if paired else lax.rem(chip + s, nch)

    def chip_from(s):
        return flip(chip, s) if paired else lax.rem(chip + nch - s, nch)

    def peer(c):
        return {"dp": c * 2 + core}

    def loop(start, stop, body):
        if stop - start <= 16:
            for s in range(start, stop):
                body(s)
        else:
            pl.loop(start, stop)(body)

    def copy(src, dst, send, recv, device):
        return pltpu.make_async_remote_copy(
            src_ref=src, dst_ref=dst, send_sem=send, recv_sem=recv, device_id=device, device_id_type=MESH)

    barrier = pltpu.get_barrier_semaphore()
    loop(1, nch, lambda s: pl.semaphore_signal(
        barrier, inc=1, device_id=peer(chip_to(nch - s)), device_id_type=MESH))
    pl.semaphore_signal(barrier, inc=1, device_id=sibling, device_id_type=MESH)

    loads = [
        pltpu.make_async_copy(cen, cbuf.at[chip, :width], ls.at[0]),
        pltpu.make_async_copy(vdir, drow, ls.at[1]),
        pltpu.make_async_copy(cnt, live, ls.at[2]),
        pltpu.make_async_copy(pts, pshare.at[core, :width], ls.at[3]),
    ]
    for load in loads:
        load.start()
    for load in loads:
        load.wait()
    cbuf[chip, width:, :] = jnp.broadcast_to(drow[...], (8, cen_dev))
    at = lax.broadcasted_iota(jnp.int32, (8, slots), 1)
    pshare[core, width:, :] = jnp.where(at < live[0], 1.0, 0.0).astype(F32)

    def send_own(s):
        return copy(cbuf.at[chip], cbuf.at[chip], gs.at[s], gr.at[chip], peer(chip_to(s)))

    share = copy(pshare.at[core], pshare.at[core], ps.at[0], ps.at[1], sibling)

    def wait_slot(q):
        copy(cbuf.at[q], cbuf.at[q], gs.at[0], gr.at[q], sibling).wait_recv()

    def exchange(part):
        return copy(ibuf.at[part, 0], ibuf.at[part, 1], es.at[part], er.at[part], sibling)

    def send_term(s):
        q = chip_to(s)
        return copy(tbuf.at[q], rbuf.at[chip], ts.at[s], tr.at[chip], peer(q))

    def one_block(q, terms, weights, half, part):
        kern = jnp.exp2(lax.dot_general(
            terms, pbuf[half, :, pl.ds(part * blk, blk)], (((0,), (0,)), ((), ())),
            preferred_element_type=F32)).astype(BF16)
        kbuf[q, half] = kern
        inn[half] += jnp.dot(weights, kern, preferred_element_type=F32)

    def stacked(q):
        held = cbuf[q]
        return stack_centres(held[:width]), rows_of(16, split3(held[width:width + 1]))

    for part in range(nblk):
        inn[...] = jnp.zeros_like(inn)
        if part == 0:
            pl.semaphore_wait(barrier, nch)
            share.start()
            loop(1, nch, lambda s: send_own(nch - s).start())
            pbuf[core] = stack_points(pshare[core, :width, :])
        one_block(chip, *stacked(chip), core, part)
        if part == 0:
            share.wait_recv()
            pbuf[other] = stack_points(pshare[other, :width, :])
        one_block(chip, *stacked(chip), other, part)

        def step(s, part=part):
            q = chip_from(s)
            if part == 0:
                wait_slot(q)
            terms, weights = stacked(q)
            one_block(q, terms, weights, 0, part)
            one_block(q, terms, weights, 1, part)

        loop(1, nch, step)

        ibuf[part, 0] = jnp.sum(inn[...], axis=1, keepdims=True)
        exchange(part).start()
        exchange(part).wait_recv()
        inner = []
        for half in range(2):
            sums = (ibuf[part, 0, half] + ibuf[part, 1, half]) * (1.0 / math.sqrt(nch * 2 * cen_dev))
            mask = pshare[half, width:width + 1, pl.ds(part * blk, blk)]
            inner.append(rows_of(16, [jnp.where(mask > 0.5, sums, 0.0)]))

        def product(q, part=part, inner=inner):
            term = 0.0
            for half in range(2):
                term = term + lax.dot_general(
                    inner[half], kbuf[q, half], (((1,), (1,)), ((), ())), preferred_element_type=F32)[:1]
            tbuf[q] = term if part == 0 else tbuf[q] + term

        def owner(s, part=part):
            product(chip_to(nch - s))
            if part == nblk - 1:
                send_term(nch - s).start()

        loop(1, nch, owner)
        product(chip)

    share.wait_send()
    loop(1, nch, lambda s: send_own(s).wait_send())
    for part in range(nblk):
        exchange(part).wait_send()
    out[...] = tbuf[chip]

    def gather(s):
        q = chip_from(s)
        copy(tbuf.at[q], rbuf.at[q], ts.at[s], tr.at[q], peer(q)).wait()
        out[...] += rbuf[q]

    loop(1, nch, gather)
    out[...] = out[...] * (1.0 / math.sqrt(slots * nch * 2))


def body(n, points, centres, direction, counts):
    width, slots = points.shape
    cen_dev = centres.shape[1]
    nch = n // 2
    nblk = 1
    while nch * cen_dev * 2 * (slots // nblk) * 2 > KERN_BYTES:
        nblk *= 2
    blk = slots // nblk
    depth = 6 * width + 16
    hbm = pl.BlockSpec(memory_space=pl.ANY)
    sem = pltpu.SemaphoreType.DMA
    got = pl.pallas_call(
        functools.partial(kernel, nch, nblk),
        out_shape=jax.ShapeDtypeStruct((1, cen_dev), F32),
        in_specs=[hbm, hbm, hbm, hbm],
        out_specs=pl.BlockSpec(memory_space=pltpu.VMEM),
        scratch_shapes=[
            pltpu.VMEM((2, width + 8, slots), F32),
            pltpu.VMEM((nch, width + 8, cen_dev), F32),
            pltpu.VMEM((1, cen_dev), F32),
            pltpu.SMEM((1,), jnp.int32),
            pltpu.VMEM((2, depth, slots), BF16),
            pltpu.VMEM((nch, 2, cen_dev, blk), BF16),
            pltpu.VMEM((2, 16, blk), F32),
            pltpu.VMEM((nblk, 2, 2, 1, blk), F32),
            pltpu.VMEM((nch, 1, cen_dev), F32),
            pltpu.VMEM((nch, 1, cen_dev), F32),
            sem((4,)), sem((2,)), sem((nch,)), sem((nch,)), sem((nblk,)), sem((nblk,)), sem((nch,)), sem((nch,)),
        ],
        compiler_params=pltpu.CompilerParams(
            collective_id=0, has_side_effects=True, vmem_limit_bytes=48 << 20),
        cost_estimate=pl.CostEstimate(
            flops=2 * slots * n * cen_dev * (depth + 2), bytes_accessed=4 * width * (slots + cen_dev),
            transcendentals=slots * n * cen_dev),
    )(points, centres, direction.reshape(1, cen_dev), counts)
    return got.reshape(cen_dev)


def solution(mesh):
    placed = (
        P(None, ("groups", "dp")),
        P(None, ("groups", "dp")),
        P(("groups", "dp")),
        P(("groups", "dp")),
    )
    return jax.shard_map(
        functools.partial(body, mesh.shape["dp"]), mesh=mesh, in_specs=placed,
        out_specs=P(("groups", "dp")), check_vma=False)
```

time: 29.1 us -> 27.9 us (0.959)
  Pallas kernels: 25.3 us -> 24.1 us
    pallas_call x1, Pallas kernels: 25.3 us -> 24.1 us  [body(): pl.pallas_call(functools.partial(kernel, nch, nblk), out_shape=jax.ShapeD...]
where the time goes in v2:
time: 27.9 us; the launch traced here: 27.7 us
  Pallas kernels  24.1 us (86%)
  local copies, waits for them, and re-layouts  2.9 us (10%)
  between operations  0.67 us (2%)
    pallas_call x1, Pallas kernels, body(): pl.pallas_call(functools.partial(kernel, nch, nblk), out_shape=jax.ShapeD...  24.1 us
    unnamed x7, local copies, waits for them, and re-layouts  2.9 us

profile of v2, /device:TPU:0, one launch (start us, length us, event | category | flops | bytes accessed | tf_op | source)
XLA Modules:
  0.0 27.7 jit_solution(16907083195615680254)
XLA Ops:
  0.7 0.0 copy-start.2
  0.7 0.7 %copy-done.2 = f32[256]{0:T(256)S(1)} copy-done((f32[256]{0:T(256)S(1)}, f32[256]{0:T(256)}, u32[]{:S(2)}) %copy-start.2) | copy-done | bytes 1048
  1.3 0.0 copy-start
  1.3 0.9 %copy-done = f32[32,1024]{1,0:T(8,128)S(1)} copy-done((f32[32,1024]{1,0:T(8,128)S(1)}, f32[32,1024]{1,0:T(8,128)}, u32[]{:S(2)}) %copy-start) | copy-done | bytes 131096
  2.2 0.0 copy-start.1
  2.2 0.8 %copy-done.1 = f32[32,256]{1,0:T(8,128)S(1)} copy-done((f32[32,256]{1,0:T(8,128)S(1)}, f32[32,256]{1,0:T(8,128)}, u32[]{:S(2)}) %copy-start.1) | copy-done | bytes 32792
  3.0 24.1 %shard_map.46 = f32[1,256]{1,0:T(1,128)S(1)} custom-call(f32[32,1024]{1,0:T(8,128)S(1)} %copy-done, f32[32,256]{1,0:T(8,128)S(1)} %copy-done.1, f32[1,256]{1,0:T(1,128)S(1)} %bitcast.3, s32[1]{0:T(128)S(6)} %copy.6.cnt), custom_call_target="tpu_custom_call" | custom-call | flops 1761607680 | bytes 163840 | tf_op jit(solution)/shard_map/pallas_call | solution.py:206
  27.1 0.6 %copy.7 = f32[256]{0:T(256)} copy(f32[256]{0:T(256)S(1)} %bitcast.2) | data formatting | bytes 2048
Async XLA Ops:
  0.7 0.7 %copy-start.2 = (f32[256]{0:T(256)S(1)}, f32[256]{0:T(256)}, u32[]{:S(2)}) copy-start(f32[256]{0:T(256)} %param.6) | copy-start | bytes 3076
  1.3 0.9 %copy-start = (f32[32,1024]{1,0:T(8,128)S(1)}, f32[32,1024]{1,0:T(8,128)}, u32[]{:S(2)}) copy-start(f32[32,1024]{1,0:T(8,128)} %pts.1) | copy-start | bytes 393220
  2.2 0.8 %copy-start.1 = (f32[32,256]{1,0:T(8,128)S(1)}, f32[32,256]{1,0:T(8,128)}, u32[]{:S(2)}) copy-start(f32[32,256]{1,0:T(8,128)} %cen.1) | copy-start | bytes 98308

commit v3 on v2

--- a/solution.py
+++ b/solution.py
@@ -46,8 +46,8 @@
     return jnp.concatenate([h, m, h, l, m, h, rows_of(16, [one, one, one, *split3(norm)])], axis=0)
 
 
-def kernel(nch, nblk, pts, cen, vdir, cnt, out, pshare, cbuf, drow, live, pbuf, kbuf, inn, ibuf, tbuf, rbuf,
-           ls, ps, gs, gr, es, er, ts, tr):
+def kernel(nch, nblk, pts, cen, vdir, cnt, out, pshare, cbuf, dbuf, live, pbuf, kbuf, inn, ibuf, tbuf, rbuf,
+           ls, ps, gs, gr, fs, ds, dr, es, er, ts, tr):
     width, slots = pts.shape
     cen_dev = cen.shape[1]
     blk = slots // nblk
@@ -91,8 +91,8 @@
     pl.semaphore_signal(barrier, inc=1, device_id=sibling, device_id_type=MESH)
 
     loads = [
-        pltpu.make_async_copy(cen, cbuf.at[chip, :width], ls.at[0]),
-        pltpu.make_async_copy(vdir, drow, ls.at[1]),
+        pltpu.make_async_copy(cen, cbuf.at[chip], ls.at[0]),
+        pltpu.make_async_copy(vdir, dbuf.at[chip], ls.at[1]),
         pltpu.make_async_copy(cnt, live, ls.at[2]),
         pltpu.make_async_copy(pts, pshare.at[core, :width], ls.at[3]),
     ]
@@ -100,17 +100,26 @@
         load.start()
     for load in loads:
         load.wait()
-    cbuf[chip, width:, :] = jnp.broadcast_to(drow[...], (8, cen_dev))
     at = lax.broadcasted_iota(jnp.int32, (8, slots), 1)
     pshare[core, width:, :] = jnp.where(at < live[0], 1.0, 0.0).astype(F32)
 
     def send_own(s):
         return copy(cbuf.at[chip], cbuf.at[chip], gs.at[s], gr.at[chip], peer(chip_to(s)))
 
+    def send_direction(s):
+        return copy(dbuf.at[chip], dbuf.at[chip], ds.at[s], dr.at[chip], peer(chip_to(s)))
+
+    def forward(s):
+        q = chip_from(s)
+        return copy(cbuf.at[q], cbuf.at[q], fs.at[s], gr.at[q], peer(chip_to(1)))
+
     share = copy(pshare.at[core], pshare.at[core], ps.at[0], ps.at[1], sibling)
 
     def wait_slot(q):
         copy(cbuf.at[q], cbuf.at[q], gs.at[0], gr.at[q], sibling).wait_recv()
+
+    def wait_direction(q):
+        copy(dbuf.at[q], dbuf.at[q], ds.at[0], dr.at[q], sibling).wait_recv()
 
     def exchange(part):
         return copy(ibuf.at[part, 0], ibuf.at[part, 1], es.at[part], er.at[part], sibling)
@@ -127,31 +136,45 @@
         inn[half] += jnp.dot(weights, kern, preferred_element_type=F32)
 
     def stacked(q):
-        held = cbuf[q]
-        return stack_centres(held[:width]), rows_of(16, split3(held[width:width + 1]))
-
+        return stack_centres(cbuf[q]), rows_of(16, split3(dbuf[q]))
+
+    direct = [s for s in range(nch) if s == 1 or s % 2 == 0][1:]
     for part in range(nblk):
         inn[...] = jnp.zeros_like(inn)
         if part == 0:
+            pbuf[core] = stack_points(pshare[core, :width, :])
             pl.semaphore_wait(barrier, nch)
+            for s in direct[1:]:
+                send_own(s).start()
+            send_own(1).start()
             share.start()
-            loop(1, nch, lambda s: send_own(nch - s).start())
-            pbuf[core] = stack_points(pshare[core, :width, :])
+            loop(1, nch, lambda s: send_direction(nch - s).start())
         one_block(chip, *stacked(chip), core, part)
         if part == 0:
             share.wait_recv()
             pbuf[other] = stack_points(pshare[other, :width, :])
         one_block(chip, *stacked(chip), other, part)
 
-        def step(s, part=part):
-            q = chip_from(s)
+        def both(q, part=part):
             if part == 0:
-                wait_slot(q)
+                wait_direction(q)
             terms, weights = stacked(q)
             one_block(q, terms, weights, 0, part)
             one_block(q, terms, weights, 1, part)
 
-        loop(1, nch, step)
+        def step(k, part=part):
+            near, far = chip_from(2 * k), chip_from(2 * k - 1)
+            if part == 0:
+                wait_slot(near)
+                forward(2 * k).start()
+                wait_slot(far)
+            both(far)
+            both(near)
+
+        loop(1, nch // 2, step)
+        if part == 0:
+            wait_slot(chip_from(nch - 1))
+        both(chip_from(nch - 1))
 
         ibuf[part, 0] = jnp.sum(inn[...], axis=1, keepdims=True)
         exchange(part).start()
@@ -178,7 +201,10 @@
         product(chip)
 
     share.wait_send()
-    loop(1, nch, lambda s: send_own(s).wait_send())
+    for s in direct:
+        send_own(s).wait_send()
+    loop(1, nch // 2, lambda k: forward(2 * k).wait_send())
+    loop(1, nch, lambda s: send_direction(s).wait_send())
     for part in range(nblk):
         exchange(part).wait_send()
     out[...] = tbuf[chip]
@@ -201,7 +227,7 @@
         nblk *= 2
     blk = slots // nblk
     depth = 6 * width + 16
-    hbm = pl.BlockSpec(memory_space=pl.ANY)
+    hbm = pl.BlockSpec(memory_space=pltpu.HBM)
     sem = pltpu.SemaphoreType.DMA
     got = pl.pallas_call(
         functools.partial(kernel, nch, nblk),
@@ -210,8 +236,8 @@
         out_specs=pl.BlockSpec(memory_space=pltpu.VMEM),
         scratch_shapes=[
             pltpu.VMEM((2, width + 8, slots), F32),
-            pltpu.VMEM((nch, width + 8, cen_dev), F32),
-            pltpu.VMEM((1, cen_dev), F32),
+            pltpu.VMEM((nch, width, cen_dev), F32),
+            pltpu.VMEM((nch, 1, cen_dev), F32),
             pltpu.SMEM((1,), jnp.int32),
             pltpu.VMEM((2, depth, slots), BF16),
             pltpu.VMEM((nch, 2, cen_dev, blk), BF16),
@@ -219,7 +245,7 @@
             pltpu.VMEM((nblk, 2, 2, 1, blk), F32),
             pltpu.VMEM((nch, 1, cen_dev), F32),
             pltpu.VMEM((nch, 1, cen_dev), F32),
-            sem((4,)), sem((2,)), sem((nch,)), sem((nch,)), sem((nblk,)), sem((nblk,)), sem((nch,)), sem((nch,)),
+            sem((4,)), sem((2,)), sem((nch,)), sem((nch,)), sem((nch,)), sem((nch,)), sem((nch,)), sem((nblk,)), sem((nblk,)), sem((nch,)), sem((nch,)),
         ],
         compiler_params=pltpu.CompilerParams(
             collective_id=0, has_side_effects=True, vmem_limit_bytes=48 << 20),

time: 27.9 us -> 28.3 us (1.014)
  Pallas kernels: 24.1 us -> 24.5 us
    pallas_call x1, Pallas kernels: 24.1 us -> 24.5 us  [body(): pl.pallas_call(functools.partial(kernel, nch, nblk), out_shape=jax.ShapeD...]
where the time goes in v3:
time: 28.3 us; the launch traced here: 28.1 us
  Pallas kernels  24.5 us (87%)
  local copies, waits for them, and re-layouts  2.9 us (10%)
  between operations  0.67 us (2%)
    pallas_call x1, Pallas kernels, body(): pl.pallas_call(functools.partial(kernel, nch, nblk), out_shape=jax.ShapeD...  24.5 us
    unnamed x7, local copies, waits for them, and re-layouts  2.9 us

profile of v3, /device:TPU:0, one launch (start us, length us, event | category | flops | bytes accessed | tf_op | source)
XLA Modules:
  0.0 28.1 jit_solution(968162805440600614)
XLA Ops:
  0.7 0.0 copy-start.2
  0.7 0.7 %copy-done.2 = f32[256]{0:T(256)S(1)} copy-done((f32[256]{0:T(256)S(1)}, f32[256]{0:T(256)}, u32[]{:S(2)}) %copy-start.2) | copy-done | bytes 1048
  1.3 0.0 copy-start
  1.3 0.9 %copy-done = f32[32,1024]{1,0:T(8,128)S(1)} copy-done((f32[32,1024]{1,0:T(8,128)S(1)}, f32[32,1024]{1,0:T(8,128)}, u32[]{:S(2)}) %copy-start) | copy-done | bytes 131096
  2.2 0.0 copy-start.1
  2.2 0.8 %copy-done.1 = f32[32,256]{1,0:T(8,128)S(1)} copy-done((f32[32,256]{1,0:T(8,128)S(1)}, f32[32,256]{1,0:T(8,128)}, u32[]{:S(2)}) %copy-start.1) | copy-done | bytes 32792
  3.0 24.5 %shard_map.46 = f32[1,256]{1,0:T(1,128)S(1)} custom-call(f32[32,1024]{1,0:T(8,128)S(1)} %copy-done, f32[32,256]{1,0:T(8,128)S(1)} %copy-done.1, f32[1,256]{1,0:T(1,128)S(1)} %bitcast.3, s32[1]{0:T(128)S(6)} %copy.6.cnt), custom_call_target="tpu_custom_call" | custom-call | flops 1761607680 | bytes 163840 | tf_op jit(solution)/shard_map/pallas_call | solution.py:232
  27.5 0.6 %copy.7 = f32[256]{0:T(256)} copy(f32[256]{0:T(256)S(1)} %bitcast.2) | data formatting | bytes 2048
Async XLA Ops:
  0.7 0.7 %copy-start.2 = (f32[256]{0:T(256)S(1)}, f32[256]{0:T(256)}, u32[]{:S(2)}) copy-start(f32[256]{0:T(256)} %param.6) | copy-start | bytes 3076
  1.3 0.9 %copy-start = (f32[32,1024]{1,0:T(8,128)S(1)}, f32[32,1024]{1,0:T(8,128)}, u32[]{:S(2)}) copy-start(f32[32,1024]{1,0:T(8,128)} %pts.1) | copy-start | bytes 393220
  2.2 0.8 %copy-start.1 = (f32[32,256]{1,0:T(8,128)S(1)}, f32[32,256]{1,0:T(8,128)}, u32[]{:S(2)}) copy-start(f32[32,256]{1,0:T(8,128)} %cen.1) | copy-start | bytes 98308

commit v4 on v3

--- a/solution.py
+++ b/solution.py
@@ -47,7 +47,7 @@
 
 
 def kernel(nch, nblk, pts, cen, vdir, cnt, out, pshare, cbuf, dbuf, live, pbuf, kbuf, inn, ibuf, tbuf, rbuf,
-           ls, ps, gs, gr, fs, ds, dr, es, er, ts, tr):
+           ls, ps, gs, gr, ds, dr, es, er, ts, tr):
     width, slots = pts.shape
     cen_dev = cen.shape[1]
     blk = slots // nblk
@@ -109,10 +109,6 @@
     def send_direction(s):
         return copy(dbuf.at[chip], dbuf.at[chip], ds.at[s], dr.at[chip], peer(chip_to(s)))
 
-    def forward(s):
-        q = chip_from(s)
-        return copy(cbuf.at[q], cbuf.at[q], fs.at[s], gr.at[q], peer(chip_to(1)))
-
     share = copy(pshare.at[core], pshare.at[core], ps.at[0], ps.at[1], sibling)
 
     def wait_slot(q):
@@ -138,16 +134,13 @@
     def stacked(q):
         return stack_centres(cbuf[q]), rows_of(16, split3(dbuf[q]))
 
-    direct = [s for s in range(nch) if s == 1 or s % 2 == 0][1:]
     for part in range(nblk):
         inn[...] = jnp.zeros_like(inn)
         if part == 0:
             pbuf[core] = stack_points(pshare[core, :width, :])
             pl.semaphore_wait(barrier, nch)
-            for s in direct[1:]:
-                send_own(s).start()
-            send_own(1).start()
             share.start()
+            loop(1, nch, lambda s: send_own(s).start())
             loop(1, nch, lambda s: send_direction(nch - s).start())
         one_block(chip, *stacked(chip), core, part)
         if part == 0:
@@ -162,19 +155,13 @@
             one_block(q, terms, weights, 0, part)
             one_block(q, terms, weights, 1, part)
 
-        def step(k, part=part):
-            near, far = chip_from(2 * k), chip_from(2 * k - 1)
+        def step(s, part=part):
+            q = chip_from(s)
             if part == 0:
-                wait_slot(near)
-                forward(2 * k).start()
-                wait_slot(far)
-            both(far)
-            both(near)
-
-        loop(1, nch // 2, step)
-        if part == 0:
-            wait_slot(chip_from(nch - 1))
-        both(chip_from(nch - 1))
+                wait_slot(q)
+            both(q)
+
+        loop(1, nch, step)
 
         ibuf[part, 0] = jnp.sum(inn[...], axis=1, keepdims=True)
         exchange(part).start()
@@ -201,9 +188,7 @@
         product(chip)
 
     share.wait_send()
-    for s in direct:
-        send_own(s).wait_send()
-    loop(1, nch // 2, lambda k: forward(2 * k).wait_send())
+    loop(1, nch, lambda s: send_own(s).wait_send())
     loop(1, nch, lambda s: send_direction(s).wait_send())
     for part in range(nblk):
         exchange(part).wait_send()
@@ -245,10 +230,10 @@
             pltpu.VMEM((nblk, 2, 2, 1, blk), F32),
             pltpu.VMEM((nch, 1, cen_dev), F32),
             pltpu.VMEM((nch, 1, cen_dev), F32),
-            sem((4,)), sem((2,)), sem((nch,)), sem((nch,)), sem((nch,)), sem((nch,)), sem((nch,)), sem((nblk,)), sem((nblk,)), sem((nch,)), sem((nch,)),
+            sem((4,)), sem((2,)), sem((nch,)), sem((nch,)), sem((nch,)), sem((nch,)), sem((nblk,)), sem((nblk,)), sem((nch,)), sem((nch,)),
         ],
         compiler_params=pltpu.CompilerParams(
-            collective_id=0, has_side_effects=True, vmem_limit_bytes=48 << 20),
+            collective_id=0, has_side_effects=True, vmem_limit_bytes=63 << 20),
         cost_estimate=pl.CostEstimate(
             flops=2 * slots * n * cen_dev * (depth + 2), bytes_accessed=4 * width * (slots + cen_dev),
             transcendentals=slots * n * cen_dev),

time: 28.3 us -> 25.7 us (0.908)
  local copies, waits for them, and re-layouts: 2.9 us -> 1.22 us
  Pallas kernels: 24.5 us -> 23.6 us
    unnamed x7 -> x3, local copies, waits for them, and re-layouts: 2.9 us -> 1.22 us
    pallas_call x1, Pallas kernels: 24.5 us -> 23.6 us  [body(): pl.pallas_call(functools.partial(kernel, nch, nblk), out_shape=jax.ShapeD...]
where the time goes in v4:
time: 25.7 us; the launch traced here: 25.5 us
  Pallas kernels  23.6 us (92%)
  local copies, waits for them, and re-layouts  1.22 us (5%)
  between operations  0.67 us (3%)
    pallas_call x1, Pallas kernels, body(): pl.pallas_call(functools.partial(kernel, nch, nblk), out_shape=jax.ShapeD...  23.6 us
    unnamed x3, local copies, waits for them, and re-layouts  1.22 us

profile of v4, /device:TPU:0, one launch (start us, length us, event | category | flops | bytes accessed | tf_op | source)
XLA Modules:
  0.0 25.5 jit_solution(2964934754939387834)
XLA Ops:
  0.7 23.6 %shard_map.46 = f32[1,256]{1,0:T(1,128)} custom-call(f32[32,1024]{1,0:T(8,128)} %pts.1, f32[32,256]{1,0:T(8,128)} %cen.1, f32[1,256]{1,0:T(1,128)} %bitcast.3, s32[1]{0:T(128)S(6)} %copy.6.cnt), custom_call_target="tpu_custom_call" | custom-call | flops 1761607680 | bytes 163840 | tf_op jit(solution)/shard_map/pallas_call | solution.py:217
  24.3 0.0 copy-start
  24.3 0.7 %copy-done = f32[1,256]{1,0:T(1,128)S(1)} copy-done((f32[1,256]{1,0:T(1,128)S(1)}, f32[1,256]{1,0:T(1,128)}, u32[]{:S(2)}) %copy-start) | copy-done | bytes 1048
  25.0 0.6 %copy.7 = f32[256]{0:T(256)} copy(f32[256]{0:T(256)S(1)} %bitcast.2) | data formatting | bytes 2048
Async XLA Ops:
  24.3 0.7 %copy-start = (f32[1,256]{1,0:T(1,128)S(1)}, f32[1,256]{1,0:T(1,128)}, u32[]{:S(2)}) copy-start(f32[1,256]{1,0:T(1,128)} %shard_map.46) | copy-start | bytes 3076

commit v5 on v4

--- a/solution.py
+++ b/solution.py
@@ -139,9 +139,10 @@
         if part == 0:
             pbuf[core] = stack_points(pshare[core, :width, :])
             pl.semaphore_wait(barrier, nch)
+            loop(1, nch, lambda s: send_direction(s).start())
+            send_own(1).start()
             share.start()
-            loop(1, nch, lambda s: send_own(s).start())
-            loop(1, nch, lambda s: send_direction(nch - s).start())
+            loop(2, nch, lambda s: send_own(s).start())
         one_block(chip, *stacked(chip), core, part)
         if part == 0:
             share.wait_recv()

time: 25.7 us -> 25 us (0.973)
  Pallas kernels: 23.6 us -> 23 us
    pallas_call x1, Pallas kernels: 23.6 us -> 23 us  [body(): pl.pallas_call(functools.partial(kernel, nch, nblk), out_shape=jax.ShapeD...]
where the time goes in v5:
time: 25 us; the launch traced here: 24.8 us
  Pallas kernels  23 us (92%)
  local copies, waits for them, and re-layouts  1.22 us (5%)
  between operations  0.67 us (3%)
    pallas_call x1, Pallas kernels, body(): pl.pallas_call(functools.partial(kernel, nch, nblk), out_shape=jax.ShapeD...  23 us
    unnamed x3, local copies, waits for them, and re-layouts  1.22 us

profile of v5, /device:TPU:0, one launch (start us, length us, event | category | flops | bytes accessed | tf_op | source)
XLA Modules:
  0.0 24.8 jit_solution(11572489853557248736)
XLA Ops:
  0.7 23.0 %shard_map.46 = f32[1,256]{1,0:T(1,128)} custom-call(f32[32,1024]{1,0:T(8,128)} %pts.1, f32[32,256]{1,0:T(8,128)} %cen.1, f32[1,256]{1,0:T(1,128)} %bitcast.3, s32[1]{0:T(128)S(6)} %copy.6.cnt), custom_call_target="tpu_custom_call" | custom-call | flops 1761607680 | bytes 163840 | tf_op jit(solution)/shard_map/pallas_call | solution.py:218
  23.6 0.0 copy-start
  23.6 0.7 %copy-done = f32[1,256]{1,0:T(1,128)S(1)} copy-done((f32[1,256]{1,0:T(1,128)S(1)}, f32[1,256]{1,0:T(1,128)}, u32[]{:S(2)}) %copy-start) | copy-done | bytes 1048
  24.3 0.6 %copy.7 = f32[256]{0:T(256)} copy(f32[256]{0:T(256)S(1)} %bitcast.2) | data formatting | bytes 2048
Async XLA Ops:
  23.6 0.7 %copy-start = (f32[1,256]{1,0:T(1,128)S(1)}, f32[1,256]{1,0:T(1,128)}, u32[]{:S(2)}) copy-start(f32[1,256]{1,0:T(1,128)} %shard_map.46) | copy-start | bytes 3076
